TPU v7x, 256 devices: a whole 4x4x8 slice. The times are simulated.
256 devices in a mesh: row: 8 (over x, y_lo), col: 32 (over z, y_hi, core).
Axes of the slice: x: 4, y: 4 (y_hi: 2, y_lo: 2; y = y_hi * 2 + y_lo), z: 8, core: 2. Of those that a mesh axis runs over, the one named last changes fastest.
Arguments:
- sigma: float32 [16384, 16384], P('col', 'row'), as said below
- factor: float32 [4096, 1024], P('row', 'col'), may hold values from -0.1875 to 0.1875
- blk_map: int32 [32], P('row'), may hold values from 0 to 127, as said below
- base_var: float32 [1024], P('col'), may hold values from 0.5 to 2
Outputs:
- cross: float32 [16384, 1024], P(('col', 'row'))
- variance: float32 [1024], P('col')
Inputs may be any that keep to these rules, and one draw needn't show every extreme that they name: `blk_map`: entries r * 4 to r * 4 + 3 name distinct parent blocks of r * 16 to r * 16 + 15 in increasing order, the last block of that range always among them. `sigma`: symmetric.
All inputs are finite; a program needn't handle non-finite values.
Results may differ from a plain program's by a relative error of at most 0.000073.
Values sent between devices are 32-bit elements; how exact they have to be, the bound alone decides.
A program may use at most 64 MiB of HBM per device.

v0:
```python
import jax
import jax.numpy as jnp
from jax import lax
from jax.sharding import PartitionSpec as P

BLK = 128


def per_device(sigma, factor, blk_map, base_var):
    own_height, own_width = sigma.shape
    range_blocks = own_width // BLK
    child_blocks = blk_map.shape[0]
    row_count_axis = lax.axis_size("row")
    row_index = lax.axis_index("row")
    col_index = lax.axis_index("col")
    row_share = own_height // row_count_axis
    local_block = blk_map % range_blocks
    front = lax.all_gather(factor, "col", axis=1, tiled=True)
    width_all = front.shape[1]
    picked = jnp.take(sigma.reshape(own_height, range_blocks, BLK), local_block, axis=1)
    picked = picked.reshape(own_height, child_blocks * BLK)
    empty = jnp.zeros((range_blocks, BLK, width_all), jnp.float32)
    lifted = empty.at[local_block].set(front.reshape(child_blocks, BLK, width_all))
    lifted = lifted.reshape(range_blocks * BLK, width_all)
    owner_row = col_index * own_height // own_width
    offset = col_index * own_height % own_width
    block_lifted = lax.dynamic_slice_in_dim(lifted, offset, own_height, 0)
    partial_panel = jnp.dot(
        picked, front, precision=lax.Precision.HIGHEST, preferred_element_type=jnp.float32
    )
    panel = lax.psum(partial_panel, "row")
    own_rows = lax.dynamic_slice_in_dim(panel, row_index * row_share, row_share, 0)
    diag_term = jnp.where(row_index == owner_row, jnp.sum(block_lifted * panel, axis=0), 0.0)
    cross = -own_rows
    col_share = base_var.shape[0]
    totals = lax.psum(diag_term, ("row", "col"))
    variance = base_var + lax.dynamic_slice_in_dim(totals, col_index * col_share, col_share, 0)
    return (cross, variance)


def solution(mesh):
    return jax.shard_map(
        per_device,
        mesh=mesh,
        in_specs=(P("col", "row"), P("row", "col"), P("row"), P("col")),
        out_specs=(P(("col", "row"), None), P("col")),
        check_vma=False,
    )
```

profile of v0, /device:TPU:1, one launch (start us, length us, event | category | flops | bytes accessed | tf_op | source)
XLA Modules:
  0.0 298.2 jit_solution(13774389751887969328)
XLA Ops:
  7.2 0.0 all-gather.2.cloned.1.call-start
  7.2 0.7 all-gather.2.cloned.1.call-update
  7.9 0.0 all-reduce.2.cloned.1.call-start
  7.9 5.4 %copy.8 = f32[512,2048]{0,1:T(8,128)} copy(f32[512,2048]{1,0:T(8,128)} %param.4) | data formatting | bytes 8388608 | tf_op args[0]
  13.3 0.0 copy-start.1
  13.3 5.3 %copy.9 = f32[512,16,128]{2,0,1:T(8,128)} copy(f32[512,16,128]{0,2,1:T(8,128)} %bitcast.11) | data formatting | bytes 8388608 | tf_op jit(solution)/shard_map/reshape | solution.py:20
  18.6 0.0 copy-done.1
  18.7 2.8 gather_fusion
  21.5 0.3 copy.10
  21.8 0.1 broadcast_bitcast_fusion
  21.9 0.1 bitcast_select_fusion
  22.0 73.0 %all-gather.2.cloned.1.call-done = f32[512,1024]{0,1:T(8,128)} async-done(((f32[512,32]{0,1:T(8,128)}), f32[512,1024]{0,1:T(8,128)}) %all-gather.2.cloned.1.call-update) | async-done | bytes 2097168 | tf_op jit(solution)/shard_map/all_gather | solution.py:18
  95.0 9.7 %fusion.1 = f32[512,1024]{1,0:T(8,128)} fusion(f32[512,512]{0,1:T(8,128)S(1)} %bitcast_select_fusion, f32[512,1024]{0,1:T(8,128)} %all-gather.2.cloned.1.call-done), kind=kOutput, calls=%fused_computation.15 | convolution fusion | flops 3221225472 | bytes 5242880 | tf_op jit(solution)/shard_map/dot_general | solution.py:28
  104.7 0.0 all-reduce.2.cloned.1.call-update
  104.7 1.9 copy.12
  106.6 4.3 %broadcast_in_dim.29 = f32[16,128,1024]{2,1,0:T(8,128)} broadcast(f32[]{:T(128)} %constant.72.clone.1), dimensions={} | broadcast | bytes 8388612 | tf_op jit(solution)/shard_map/broadcast_in_dim | solution.py:22
  110.9 3.7 %scatter_fusion = f32[16,128,1024]{2,1,0:T(8,128)} fusion(f32[16,128,1024]{2,1,0:T(8,128)} %broadcast_in_dim.29, s32[4]{0:T(128)S(1)} %get-tuple-element.3, f32[4,128,1024]{2,1,0:T(8,128)S(1)} %bitcast.12), kind=kCustom, calls=%fused_computation.1 | custom fusion | bytes 6291472 | tf_op jit(solution)/shard_map/scatter | solution.py:23
  114.7 95.0 %all-reduce.2.cloned.1.call-done = f32[512,1024]{1,0:T(8,128)} async-done(((f32[512,1024]{1,0:T(8,128)}), f32[512,1024]{1,0:T(8,128)}) %all-reduce.2.cloned.1.call-update) | async-done | bytes 2097168 | tf_op jit(solution)/shard_map/psum | solution.py:31
  209.6 0.0 copy-start
  209.6 2.5 multiply_reduce_fusion
  212.1 77.0 %psum.15 = f32[1024]{0:T(1024)S(1)} all-reduce(f32[1024]{0:T(1024)S(1)} %broadcast_select_fusion), channel_id=1, replica_groups=mesh['row'=8,'col'=32] {'row','col'}, use_global_device_ids=true, to_apply=%region_3.4 | all-reduce | flops 1024 | bytes 8192 | tf_op jit(solution)/shard_map/psum | solution.py:36
  289.1 0.0 copy-done
  289.1 0.6 dynamic-slice_add_fusion
  289.7 1.7 dynamic-slice_negate_fusion
  (3 shorter events, 0.0 us)
Async XLA Ops:
  7.2 87.8 %all-gather.2.cloned.1.call-start = ((), (), s32[]{:S(2)}) async-start(), calls=%async_computation | async-start | bytes 2162688 | tf_op jit(solution)/shard_map/all_gather | solution.py:18
  7.9 201.7 %all-reduce.2.cloned.1.call-start = ((), (), s32[]{:S(2)}) async-start(), calls=%async_computation.1 | async-start | bytes 4194304 | tf_op jit(solution)/shard_map/psum | solution.py:31
  13.3 5.3 %copy-start.1 = (s32[4]{0:T(128)S(1)}, s32[4]{0:T(128)}, u32[]{:S(2)}) copy-start(s32[4]{0:T(128)} %param.6) | copy-start | bytes 52
  209.6 79.5 %copy-start = (f32[32]{0:T(128)S(1)}, f32[32]{0:T(128)}, u32[]{:S(2)}) copy-start(f32[32]{0:T(128)} %param.7) | copy-start | bytes 388
Sparse Core Ops, SparseCore 0:
  10.8 84.1 all-gather.1
  104.8 104.7 all-reduce.1
where the time goes:
time: 299 us; the launch traced here: 298 us
  waiting for transfers between devices  169 us (57%)
  blocking collectives  77 us (26%)
  local copies, waits for them, and re-layouts  23.9 us (8%)
  between operations  14.1 us (5%)
  matrix products  9.66 us (3%)
  other arithmetic  4.9 us (2%)
    psum x1, waiting for transfers between devices, per_device(): panel = lax.psum(partial_panel, 'row')  95 us
    psum x1, blocking collectives, per_device(): totals = lax.psum(diag_term, ('row', 'col'))  77 us
    all_gather x1, waiting for transfers between devices, per_device(): front = lax.all_gather(factor, 'col', axis=1, tiled=True)  73 us
    dot_general x1, matrix products, per_device(): jnp.dot(picked, front, precision=lax.Precision.HIGHEST, preferred_element...  9.66 us
  transfers between devices with their start and end apart: 2, of which 2 were waited for; matrix products, arithmetic and copies ran while one was open for 8% of the time, Pallas kernels for 0%

commit v1 on v0

v1 whole, which is shorter than its diff:
```python
import functools

import jax
import jax.numpy as jnp
from jax import lax
from jax.experimental import pallas as pl
from jax.experimental.pallas import tpu as pltpu
from jax.sharding import PartitionSpec as P

MESH = pl.DeviceIdType.MESH
BLK = 128
POS = {0: 0, 4: 1, 1: 2, 7: 3, 2: 4, 6: 5, 3: 6, 5: 7}
XFIRST = (1, 2, 3, 0)


def kernel(
    sig_hbm, fact_ref, blk_ref, base_ref, out_ref, var_ref,
    sig, acat, front, part, xr, yr, stage, ls_src, ls1, lift, sv, va, vb_src, vb,
    sig_sem, agz_s, agz_r, yh_s, yh_r, sib_s, sib_r, l1_s, l1_r, l2_s, l2_r,
    x_s, x_r, y_s, y_r, va_s, va_r, vb_s, vb_r,
):
    r = lax.axis_index("row")
    c = lax.axis_index("col")
    x, yl = r // 2, r % 2
    z, yh, co = c // 4, (c // 2) % 2, c % 2
    k = c % 4

    def dev(dx=0, dy=0, dz=0, dh=0, dc=0):
        return (
            ((x + dx) % 4) * 2 + (yl + dy) % 2,
            ((z + dz) % 8) * 4 + ((yh + dh) % 2) * 2 + (co + dc) % 2,
        )

    def send(src, dst, ssem, rsem, to):
        cp = pltpu.make_async_remote_copy(
            src, dst, ssem, rsem, device_id=to, device_id_type=MESH
        )
        cp.start()
        return cp

    pending = []

    def push(*args):
        cp = send(*args)
        pending.append(cp)
        return cp

    cp_sig = pltpu.make_async_copy(sig_hbm, sig, sig_sem)
    cp_sig.start()
    plane = [
        (dx, dy, dh, dc)
        for dx in range(4) for dy in range(2) for dh in range(2) for dc in range(2)
    ][1:]
    barrier = pltpu.get_barrier_semaphore()
    for dx, dy, dh, dc in plane:
        pl.semaphore_signal(barrier, inc=1, device_id=dev(dx, dy, 0, dh, dc), device_id_type=MESH)
    for dz in range(1, 8):
        pl.semaphore_signal(barrier, inc=1, device_id=dev(dz=dz), device_id_type=MESH)

    def rows(op):
        src_k = k if op == 0 else ((yh + 1) % 2) * 2 + co
        return pl.ds(pl.multiple_of(src_k * 32, 32), 32)

    def piece(d, op):
        return front.at[POS[d], rows(op)]

    front[POS[0], rows(0), :] = fact_ref[...]
    cp_sig.wait()
    def pick(step, carry):
        at = pl.ds(pl.multiple_of(step * 32, 32), 32)
        for i in range(4):
            if i == 3:
                a = sig[at, 15 * BLK:16 * BLK]
            else:
                where = jnp.full((32, BLK), blk_ref[i] - r * 16, jnp.int32)
                a = sig[at, i * BLK:(i + 1) * BLK]
                for b in range(i + 1, i + 13):
                    a = jnp.where(where == b, sig[at, b * BLK:(b + 1) * BLK], a)
            hi = a.astype(jnp.bfloat16)
            lo = (a - hi.astype(jnp.float32)).astype(jnp.bfloat16)
            acat[at, i * BLK:(i + 1) * BLK] = hi
            acat[at, 512 + i * BLK:512 + (i + 1) * BLK] = hi
            acat[at, 1024 + i * BLK:1024 + (i + 1) * BLK] = lo
        return carry

    lax.fori_loop(0, 16, pick, 0)

    pl.semaphore_wait(barrier, len(plane) + 7)

    zcp = {}

    def zsend(d, op):
        for side, (dz, nd) in enumerate(((1, d + 1), (-1, (d - 1) % 8))):
            if d != 0 and (side == 0) != (d < 4):
                continue
            if nd == 4 and op != side:
                continue
            slot = nd * 2 + op
            zcp[nd, op] = push(piece(d, op), piece(nd, op), agz_s.at[slot], agz_r.at[slot], dev(dz=dz))

    sibcp = {}

    def sibsend(d, op):
        slot = d * 2 + op
        sibcp[d, op] = push(piece(d, op), piece(d, op), sib_s.at[slot], sib_r.at[slot], dev(dc=1))

    def arrive(d, op):
        zcp[d, op].wait_recv()
        if d != 4:
            zsend(d, op)
        sibsend(d, op)

    zsend(0, 0)
    cp_yh = push(front.at[POS[0], rows(0)], front.at[POS[0], rows(0)], yh_s, yh_r, dev(dh=1))
    sibsend(0, 0)
    arrive(1, 0)
    arrive(7, 0)
    cp_yh.wait_recv()
    zsend(0, 1)
    sibsend(0, 1)

    def sibwait(d):
        sibcp[d, 0].wait_recv()
        sibcp[d, 1].wait_recv()

    sibwait(0)
    ft = [front[POS[0], :, i * BLK:(i + 1) * BLK].T for i in range(4)]
    for b in range(4):
        blk = jnp.zeros((BLK, BLK), jnp.float32)
        for i in range(4):
            where = jnp.full((BLK, BLK), blk_ref[i] - r * 16, jnp.int32)
            blk = jnp.where(where == k * 4 + b, ft[i], blk)
        ls_src[2 * b] = blk[:64]
        ls_src[2 * b + 1] = blk[64:]
    l1 = []
    for dx in range(4):
        for dy in range(2):
            if dx + dy == 0:
                continue
            i = dx * 2 + dy
            to = dev(dx, dy)
            l1.append(push(ls_src.at[to[0]], ls1.at[r], l1_s.at[i], l1_r.at[i], to))
    ls1[r] = ls_src[r]

    cps = {}

    def rs_start(ds):
        n = len(ds)
        f = front[POS[ds[0]]:POS[ds[0]] + n].reshape(n * BLK, 512)
        hi = f.astype(jnp.bfloat16)
        lo = (f - hi.astype(jnp.float32)).astype(jnp.bfloat16)
        fcat = jnp.concatenate([hi, lo, hi], axis=1)
        res = lax.dot_general(
            acat[...], fcat, (((1,), (1,)), ((), ())), preferred_element_type=jnp.float32
        )
        for m, d in enumerate(ds):
            part[d] = res[:, m * BLK:(m + 1) * BLK].reshape(4, 2, 64, BLK)
        for d in ds:
            if d in XFIRST:
                for dx in range(1, 4):
                    cps[d, "x", dx] = push(
                        part.at[d, (x + dx) % 4], xr.at[d, dx - 1],
                        x_s.at[d * 3 + dx - 1], x_r.at[d * 3 + dx - 1], dev(dx=dx))
            else:
                cps[d, "y"] = push(part.at[d, :, 1 - yl], yr.at[d], y_s.at[d], y_r.at[d], dev(dy=1))

    def rs_mid(d):
        if d in XFIRST:
            for dx in range(1, 4):
                cps[d, "x", dx].wait_recv()
            stage[d, 0:2] = part[d, x] + xr[d, 0] + xr[d, 1] + xr[d, 2]
            cps[d, "y"] = push(stage.at[d, 1 - yl], yr.at[d, 0], y_s.at[d], y_r.at[d], dev(dy=1))
        else:
            cps[d, "y"].wait_recv()
            stage[d] = part[d, :, yl] + yr[d]
            for dx in range(1, 4):
                cps[d, "x", dx] = push(
                    stage.at[d, (x + dx) % 4], xr.at[d, dx - 1, 0],
                    x_s.at[d * 3 + dx - 1], x_r.at[d * 3 + dx - 1], dev(dx=dx))

    vacp = {}

    def rs_end(d):
        if d in XFIRST:
            cps[d, "y"].wait_recv()
            panel = stage[d, yl] + yr[d, 0]
        else:
            for dx in range(1, 4):
                cps[d, "x", dx].wait_recv()
            panel = stage[d, x] + xr[d, 0, 0] + xr[d, 1, 0] + xr[d, 2, 0]
        j = (z - d) % 8
        out_ref[:, pl.ds(pl.multiple_of(j * BLK, BLK), BLK)] = panel
        if d:
            l2cp[d].wait_recv()
        s = jnp.sum((panel * lift[d]).reshape(8, 8, BLK), axis=0)
        if d:
            sv[d] = s
            vacp[d] = push(sv.at[d], va.at[d], va_s.at[d], va_r.at[d], dev(dz=-d))
        else:
            va[0] = s

    arrive(2, 0)
    arrive(6, 0)
    arrive(1, 1)
    arrive(7, 1)
    sibwait(1)
    sibwait(7)
    rs_start((1, 7))
    arrive(3, 0)
    arrive(5, 0)
    arrive(2, 1)
    arrive(6, 1)
    sibwait(2)
    sibwait(6)
    rs_start((2, 6))
    for cp in l1:
        cp.wait_recv()
    l2cp = {}
    for dz in range(1, 8):
        l2cp[dz] = push(ls1.at[(z + dz) % 8], lift.at[dz], l2_s.at[dz], l2_r.at[dz], dev(dz=dz))
    lift[0] = ls1[z]
    rs_mid(1)
    rs_mid(7)
    arrive(4, 0)
    arrive(3, 1)
    arrive(5, 1)
    sibwait(3)
    sibwait(5)
    rs_start((3, 5))
    rs_mid(2)
    rs_mid(6)
    rs_end(1)
    rs_end(7)
    arrive(4, 1)
    sibwait(4)
    rs_start((4,))
    rs_start((0,))
    rs_mid(3)
    rs_mid(5)
    rs_end(2)
    rs_end(6)
    rs_mid(4)
    rs_mid(0)
    rs_end(3)
    rs_end(5)
    rs_end(4)
    rs_end(0)

    for d in range(1, 8):
        vacp[d].wait_recv()
    total = va[0]
    for d in range(1, 8):
        total = total + va[d]
    vb_src[...] = total
    vbcp = []
    for i, (dx, dy, dh, dc) in enumerate(plane):
        vbcp.append(push(vb_src, vb.at[i], vb_s.at[i], vb_r.at[i], dev(dx, dy, 0, dh, dc)))
    for cp in vbcp:
        cp.wait_recv()
    total = jnp.sum(total + jnp.sum(vb[...], axis=0), axis=0, keepdims=True)
    own = total[:, 0:32]
    for kk in range(1, 4):
        own = jnp.where(k == kk, total[:, kk * 32:kk * 32 + 32], own)
    var_ref[...] = base_ref[...] + own
    for cp in pending:
        cp.wait_send()


def per_device(sigma, factor, blk_map, base_var):
    f32 = jnp.float32
    vm = lambda *s: pltpu.VMEM(s, f32)
    dma = lambda n: pltpu.SemaphoreType.DMA((n,))
    vmem = pl.BlockSpec(memory_space=pltpu.VMEM)
    panel, var = pl.pallas_call(
        kernel,
        out_shape=(jax.ShapeDtypeStruct((64, 1024), f32), jax.ShapeDtypeStruct((1, 32), f32)),
        in_specs=[
            pl.BlockSpec(memory_space=pl.ANY), vmem, pl.BlockSpec(memory_space=pltpu.SMEM), vmem,
        ],
        out_specs=(vmem, vmem),
        scratch_shapes=[
            vm(512, 2048), pltpu.VMEM((512, 1536), jnp.bfloat16), vm(8, 128, 512),
            vm(8, 4, 2, 64, 128), vm(8, 3, 2, 64, 128), vm(8, 4, 64, 128), vm(8, 4, 64, 128),
            vm(8, 64, 128), vm(8, 64, 128), vm(8, 64, 128),
            vm(8, 8, 128), vm(8, 8, 128), vm(8, 128), vm(31, 8, 128),
            pltpu.SemaphoreType.DMA,
            dma(16), dma(16), pltpu.SemaphoreType.DMA, pltpu.SemaphoreType.DMA, dma(16), dma(16),
            dma(8), dma(8), dma(8), dma(8),
            dma(24), dma(24), dma(8), dma(8), dma(8), dma(8), dma(31), dma(31),
        ],
        compiler_params=pltpu.CompilerParams(
            collective_id=0, has_side_effects=True, vmem_limit_bytes=56 * 2**20
        ),
    )(sigma, factor.T, blk_map, base_var.reshape(1, 32))
    return -panel, var.reshape(32)


def solution(mesh):
    return jax.shard_map(
        per_device,
        mesh=mesh,
        in_specs=(P("col", "row"), P("row", "col"), P("row"), P("col")),
        out_specs=(P(("col", "row"), None), P("col")),
        check_vma=False,
    )
```

time: 299 us -> 61.7 us (0.21)
  waiting for transfers between devices: 169 us -> 0 us
  blocking collectives: 77 us -> 0 us
  Pallas kernels: 0 us -> 58 us
  local copies, waits for them, and re-layouts: 23.9 us -> 1.13 us
  between operations: 14.1 us -> 0.64 us
  matrix products: 9.66 us -> 0 us
  other arithmetic: 4.9 us -> 1.67 us
    psum x1 -> x0, waiting for transfers between devices: 95 us -> none  [per_device(): panel = lax.psum(partial_panel, 'row')]
    psum x1 -> x0, blocking collectives: 77 us -> none  [per_device(): totals = lax.psum(diag_term, ('row', 'col'))]
    all_gather x1 -> x0, waiting for transfers between devices: 73 us -> none  [per_device(): front = lax.all_gather(factor, 'col', axis=1, tiled=True)]
    pallas_call x0 -> x1, Pallas kernels: none -> 58 us  [per_device(): pl.pallas_call(kernel, out_shape=(jax.ShapeDtypeStruct((64, 1024), f32),...]
    dot_general x1 -> x0, matrix products: 9.66 us -> none  [per_device(): jnp.dot(picked, front, precision=lax.Precision.HIGHEST, preferred_element...]
    reshape x2 -> x0, local copies, waits for them, and re-layouts: 7.25 us -> none  [the longest x1 5.32 us: per_device(): sigma.reshape(own_height, range_blocks, BLK)]
    broadcast_in_dim x2 -> x0, local copies, waits for them, and re-layouts: 4.36 us -> none  [the longest x1 4.29 us: per_device(): empty = jnp.zeros((range_blocks, BLK, width_all), jnp.float32)]
    unnamed x5 -> x1, local copies, waits for them, and re-layouts: 5.37 us -> 1.13 us
  transfers between devices with their start and end apart: 2 -> 0, of which waited for: 2 -> 0; matrix products, arithmetic and copies ran while one was open for 8% -> 0% of each run, Pallas kernels for 0% -> 0%
where the time goes in v1:
time: 61.7 us; the launch traced here: 61.5 us
  Pallas kernels  58 us (94%)
  other arithmetic  1.67 us (3%)
  local copies, waits for them, and re-layouts  1.13 us (2%)
  between operations  0.64 us (1%)
    pallas_call x1, Pallas kernels, per_device(): pl.pallas_call(kernel, out_shape=(jax.ShapeDtypeStruct((64, 1024), f32),...  58 us
    neg x1, other arithmetic, per_device(): return (-panel, var.reshape(32))  1.67 us

profile of v1, /device:TPU:1, one launch (start us, length us, event | category | flops | bytes accessed | tf_op | source)
XLA Modules:
  0.0 61.5 jit_solution(3506302602113881202)
XLA Ops:
  0.6 58.0 %shard_map.59 = (f32[64,1024]{1,0:T(8,128)}, f32[1,32]{1,0:T(1,128)}) custom-call(f32[512,2048]{1,0:T(8,128)} %sig_hbm.1, f32[32,512]{1,0:T(8,128)} %bitcast.3, s32[4]{0:T(128)} %blk_ref.1, f32[1,32]{1,0:T(1,128)} %bitcast.4), custom_call_target="tpu_custom_call" | custom-call | tf_op jit(solution)/shard_map/pallas_call | solution.py:274
  58.6 1.7 %neg.3 = f32[64,1024]{1,0:T(8,128)} negate(f32[64,1024]{1,0:T(8,128)} %get-tuple-element.4) | non-fusion elementwise | flops 65536 | bytes 524288 | tf_op jit(solution)/shard_map/neg | solution.py:295
  60.3 1.1 %copy.7 = f32[32]{0:T(128)} copy(f32[32]{0:T(128)} %bitcast.5) | data formatting | bytes 256

commit v2 on v1

--- a/solution.py
+++ b/solution.py
@@ -10,14 +10,15 @@
 MESH = pl.DeviceIdType.MESH
 BLK = 128
 POS = {0: 0, 4: 1, 1: 2, 7: 3, 2: 4, 6: 5, 3: 6, 5: 7}
-XFIRST = (1, 2, 3, 0)
+XFIRST = (1, 2, 3)
 
 
 def kernel(
-    sig_hbm, fact_ref, blk_ref, base_ref, out_ref, var_ref,
+    sig_hbm, fact_hbm, blk_ref, out_hbm, var_ref,
+    pan, in_sem, out_sem,
     sig, acat, front, part, xr, yr, stage, ls_src, ls1, lift, sv, va, vb_src, vb,
     sig_sem, agz_s, agz_r, yh_s, yh_r, sib_s, sib_r, l1_s, l1_r, l2_s, l2_r,
-    x_s, x_r, y_s, y_r, va_s, va_r, vb_s, vb_r,
+    x_s, x_r, y_s, y_r, va_s, va_r, vb_s, vb_r, dr, d_s, d_r,
 ):
     r = lax.axis_index("row")
     c = lax.axis_index("col")
@@ -45,17 +46,17 @@
         pending.append(cp)
         return cp
 
-    cp_sig = pltpu.make_async_copy(sig_hbm, sig, sig_sem)
-    cp_sig.start()
-    plane = [
+    everyone = [
         (dx, dy, dh, dc)
         for dx in range(4) for dy in range(2) for dh in range(2) for dc in range(2)
-    ][1:]
+    ]
+    plane = everyone[1:]
     barrier = pltpu.get_barrier_semaphore()
-    for dx, dy, dh, dc in plane:
-        pl.semaphore_signal(barrier, inc=1, device_id=dev(dx, dy, 0, dh, dc), device_id_type=MESH)
-    for dz in range(1, 8):
-        pl.semaphore_signal(barrier, inc=1, device_id=dev(dz=dz), device_id_type=MESH)
+    peers = [dev(dx, dy) for dx in range(4) for dy in range(2)][1:]
+    peers += [dev(dh=1), dev(dc=1)]
+    peers += [dev(dz=dz, dh=dh) for dz in (1, -1) for dh in (0, 1)]
+    for to in peers:
+        pl.semaphore_signal(barrier, inc=1, device_id=to, device_id_type=MESH)
 
     def rows(op):
         src_k = k if op == 0 else ((yh + 1) % 2) * 2 + co
@@ -64,7 +65,10 @@
     def piece(d, op):
         return front.at[POS[d], rows(op)]
 
-    front[POS[0], rows(0), :] = fact_ref[...]
+    cp_fact = pltpu.make_async_copy(fact_hbm, piece(0, 0), in_sem.at[0])
+    cp_fact.start()
+    cp_sig = pltpu.make_async_copy(sig_hbm, sig, sig_sem)
+    cp_sig.start()
     cp_sig.wait()
     def pick(step, carry):
         at = pl.ds(pl.multiple_of(step * 32, 32), 32)
@@ -85,7 +89,7 @@
 
     lax.fori_loop(0, 16, pick, 0)
 
-    pl.semaphore_wait(barrier, len(plane) + 7)
+    pl.semaphore_wait(barrier, len(peers))
 
     zcp = {}
 
@@ -110,37 +114,43 @@
             zsend(d, op)
         sibsend(d, op)
 
+    cp_fact.wait()
     zsend(0, 0)
-    cp_yh = push(front.at[POS[0], rows(0)], front.at[POS[0], rows(0)], yh_s, yh_r, dev(dh=1))
+    own = piece(0, 0)
+    for d, dz in ((1, 1), (7, -1)):
+        slot = d * 2 + 1
+        zcp[d, 1] = push(own, front.at[POS[d], rows(0)], agz_s.at[slot], agz_r.at[slot], dev(dz=dz, dh=1))
+    cp_yh = push(own, own, yh_s, yh_r, dev(dh=1))
     sibsend(0, 0)
     arrive(1, 0)
     arrive(7, 0)
     cp_yh.wait_recv()
-    zsend(0, 1)
     sibsend(0, 1)
 
     def sibwait(d):
         sibcp[d, 0].wait_recv()
         sibcp[d, 1].wait_recv()
 
-    sibwait(0)
-    ft = [front[POS[0], :, i * BLK:(i + 1) * BLK].T for i in range(4)]
-    for b in range(4):
-        blk = jnp.zeros((BLK, BLK), jnp.float32)
-        for i in range(4):
-            where = jnp.full((BLK, BLK), blk_ref[i] - r * 16, jnp.int32)
-            blk = jnp.where(where == k * 4 + b, ft[i], blk)
-        ls_src[2 * b] = blk[:64]
-        ls_src[2 * b + 1] = blk[64:]
     l1 = []
-    for dx in range(4):
-        for dy in range(2):
-            if dx + dy == 0:
-                continue
-            i = dx * 2 + dy
-            to = dev(dx, dy)
-            l1.append(push(ls_src.at[to[0]], ls1.at[r], l1_s.at[i], l1_r.at[i], to))
-    ls1[r] = ls_src[r]
+    l2cp = {}
+
+    def lift_start():
+        ft = [front[POS[0], :, i * BLK:(i + 1) * BLK].T for i in range(4)]
+        for b in range(4):
+            blk = jnp.zeros((BLK, BLK), jnp.float32)
+            for i in range(4):
+                where = jnp.full((BLK, BLK), blk_ref[i] - r * 16, jnp.int32)
+                blk = jnp.where(where == k * 4 + b, ft[i], blk)
+            ls_src[2 * b] = blk[:64]
+            ls_src[2 * b + 1] = blk[64:]
+        for dx in range(4):
+            for dy in range(2):
+                if dx + dy == 0:
+                    continue
+                i = dx * 2 + dy
+                to = dev(dx, dy)
+                l1.append(push(ls_src.at[to[0]], ls1.at[r], l1_s.at[i], l1_r.at[i], to))
+        ls1[r] = ls_src[r]
 
     cps = {}
 
@@ -156,7 +166,14 @@
         for m, d in enumerate(ds):
             part[d] = res[:, m * BLK:(m + 1) * BLK].reshape(4, 2, 64, BLK)
         for d in ds:
-            if d in XFIRST:
+            if d == 4:
+                for dx in range(4):
+                    for dy in range(2):
+                        if dx + dy:
+                            i = dx * 2 + dy - 1
+                            to = dev(dx, dy)
+                            cps[d, i] = push(part.at[d, to[0] // 2, to[0] % 2], dr.at[i], d_s.at[i], d_r.at[i], to)
+            elif d in XFIRST:
                 for dx in range(1, 4):
                     cps[d, "x", dx] = push(
                         part.at[d, (x + dx) % 4], xr.at[d, dx - 1],
@@ -179,9 +196,15 @@
                     x_s.at[d * 3 + dx - 1], x_r.at[d * 3 + dx - 1], dev(dx=dx))
 
     vacp = {}
+    outs = []
 
     def rs_end(d):
-        if d in XFIRST:
+        if d == 4:
+            panel = part[d, x, yl]
+            for i in range(7):
+                cps[d, i].wait_recv()
+                panel = panel + dr[i]
+        elif d in XFIRST:
             cps[d, "y"].wait_recv()
             panel = stage[d, yl] + yr[d, 0]
         else:
@@ -189,7 +212,11 @@
                 cps[d, "x", dx].wait_recv()
             panel = stage[d, x] + xr[d, 0, 0] + xr[d, 1, 0] + xr[d, 2, 0]
         j = (z - d) % 8
-        out_ref[:, pl.ds(pl.multiple_of(j * BLK, BLK), BLK)] = panel
+        pan[d] = panel
+        cp = pltpu.make_async_copy(
+            pan.at[d], out_hbm.at[:, pl.ds(pl.multiple_of(j * BLK, BLK), BLK)], out_sem.at[d])
+        cp.start()
+        outs.append(cp)
         if d:
             l2cp[d].wait_recv()
         s = jnp.sum((panel * lift[d]).reshape(8, 8, BLK), axis=0)
@@ -199,57 +226,53 @@
         else:
             va[0] = s
 
+    def start(*ds):
+        for d in ds:
+            sibwait(d)
+        rs_start(ds)
+
+    start(0)
+    arrive(1, 1)
+    arrive(7, 1)
+    lift_start()
     arrive(2, 0)
     arrive(6, 0)
-    arrive(1, 1)
-    arrive(7, 1)
-    sibwait(1)
-    sibwait(7)
-    rs_start((1, 7))
+    start(1, 7)
+    arrive(2, 1)
+    arrive(6, 1)
     arrive(3, 0)
     arrive(5, 0)
-    arrive(2, 1)
-    arrive(6, 1)
-    sibwait(2)
-    sibwait(6)
-    rs_start((2, 6))
+    start(2, 6)
+    rs_mid(0)
+    arrive(3, 1)
+    arrive(5, 1)
+    arrive(4, 0)
+    start(3, 5)
+    rs_mid(1)
+    rs_mid(7)
+    arrive(4, 1)
+    start(4)
     for cp in l1:
         cp.wait_recv()
-    l2cp = {}
     for dz in range(1, 8):
         l2cp[dz] = push(ls1.at[(z + dz) % 8], lift.at[dz], l2_s.at[dz], l2_r.at[dz], dev(dz=dz))
     lift[0] = ls1[z]
-    rs_mid(1)
-    rs_mid(7)
-    arrive(4, 0)
-    arrive(3, 1)
-    arrive(5, 1)
-    sibwait(3)
-    sibwait(5)
-    rs_start((3, 5))
     rs_mid(2)
     rs_mid(6)
+    rs_mid(3)
+    rs_mid(5)
+    rs_end(0)
     rs_end(1)
     rs_end(7)
-    arrive(4, 1)
-    sibwait(4)
-    rs_start((4,))
-    rs_start((0,))
-    rs_mid(3)
-    rs_mid(5)
     rs_end(2)
     rs_end(6)
-    rs_mid(4)
-    rs_mid(0)
+    rs_end(4)
     rs_end(3)
     rs_end(5)
-    rs_end(4)
-    rs_end(0)
-
+
+    total = va[0]
     for d in range(1, 8):
         vacp[d].wait_recv()
-    total = va[0]
-    for d in range(1, 8):
         total = total + va[d]
     vb_src[...] = total
     vbcp = []
@@ -257,13 +280,21 @@
         vbcp.append(push(vb_src, vb.at[i], vb_s.at[i], vb_r.at[i], dev(dx, dy, 0, dh, dc)))
     for cp in vbcp:
         cp.wait_recv()
-    total = jnp.sum(total + jnp.sum(vb[...], axis=0), axis=0, keepdims=True)
+    total = total + jnp.sum(vb[...], axis=0)
+    total = jnp.sum(total, axis=0, keepdims=True)
     own = total[:, 0:32]
     for kk in range(1, 4):
         own = jnp.where(k == kk, total[:, kk * 32:kk * 32 + 32], own)
-    var_ref[...] = base_ref[...] + own
+    var_ref[...] = own
+    for cp in outs:
+        cp.wait()
     for cp in pending:
         cp.wait_send()
+
+
+def finish(panel_ref, terms_ref, base_ref, cross_ref, var_ref):
+    cross_ref[...] = -panel_ref[...]
+    var_ref[...] = base_ref[...] + terms_ref[...]
 
 
 def per_device(sigma, factor, blk_map, base_var):
@@ -271,14 +302,14 @@
     vm = lambda *s: pltpu.VMEM(s, f32)
     dma = lambda n: pltpu.SemaphoreType.DMA((n,))
     vmem = pl.BlockSpec(memory_space=pltpu.VMEM)
+    hbm = pl.BlockSpec(memory_space=pl.ANY)
     panel, var = pl.pallas_call(
         kernel,
         out_shape=(jax.ShapeDtypeStruct((64, 1024), f32), jax.ShapeDtypeStruct((1, 32), f32)),
-        in_specs=[
-            pl.BlockSpec(memory_space=pl.ANY), vmem, pl.BlockSpec(memory_space=pltpu.SMEM), vmem,
-        ],
-        out_specs=(vmem, vmem),
+        in_specs=[hbm, hbm, pl.BlockSpec(memory_space=pltpu.SMEM)],
+        out_specs=(hbm, vmem),
         scratch_shapes=[
+            vm(8, 64, 128), dma(2), dma(8),
             vm(512, 2048), pltpu.VMEM((512, 1536), jnp.bfloat16), vm(8, 128, 512),
             vm(8, 4, 2, 64, 128), vm(8, 3, 2, 64, 128), vm(8, 4, 64, 128), vm(8, 4, 64, 128),
             vm(8, 64, 128), vm(8, 64, 128), vm(8, 64, 128),
@@ -287,12 +318,19 @@
             dma(16), dma(16), pltpu.SemaphoreType.DMA, pltpu.SemaphoreType.DMA, dma(16), dma(16),
             dma(8), dma(8), dma(8), dma(8),
             dma(24), dma(24), dma(8), dma(8), dma(8), dma(8), dma(31), dma(31),
+            vm(7, 64, 128), dma(7), dma(7),
         ],
         compiler_params=pltpu.CompilerParams(
             collective_id=0, has_side_effects=True, vmem_limit_bytes=56 * 2**20
         ),
-    )(sigma, factor.T, blk_map, base_var.reshape(1, 32))
-    return -panel, var.reshape(32)
+    )(sigma, factor.T, blk_map)
+    cross, var = pl.pallas_call(
+        finish,
+        out_shape=(jax.ShapeDtypeStruct((64, 1024), f32), jax.ShapeDtypeStruct((1, 32), f32)),
+        in_specs=[vmem] * 3,
+        out_specs=(vmem, vmem),
+    )(panel, var, base_var.reshape(1, 32))
+    return cross, var.reshape(32)
 
 
 def solution(mesh):

time: 61.7 us -> 56.4 us (0.914)
  Pallas kernels: 58 us -> 55.6 us
  other arithmetic: 1.67 us -> 0 us
  local copies, waits for them, and re-layouts: 1.13 us -> 0 us
    pallas_call x1, Pallas kernels: 58 us -> 53.9 us  [per_device(): pl.pallas_call(kernel, out_shape=(jax.ShapeDtypeStruct((64, 1024), f32),...]
    pallas_call x0 -> x1, Pallas kernels: none -> 1.68 us  [per_device(): pl.pallas_call(finish, out_shape=(jax.ShapeDtypeStruct((64, 1024), f32),...]
    neg x1 -> x0, other arithmetic: 1.67 us -> none  [per_device(): return (-panel, var.reshape(32))]
    unnamed x1 -> x0, local copies, waits for them, and re-layouts: 1.13 us -> none
where the time goes in v2:
time: 56.4 us; the launch traced here: 56.2 us
  Pallas kernels  55.6 us (99%)
  between operations  0.64 us (1%)
    pallas_call x1, Pallas kernels, per_device(): pl.pallas_call(kernel, out_shape=(jax.ShapeDtypeStruct((64, 1024), f32),...  53.9 us
    pallas_call x1, Pallas kernels, per_device(): pl.pallas_call(finish, out_shape=(jax.ShapeDtypeStruct((64, 1024), f32),...  1.68 us

profile of v2, /device:TPU:1, one launch (start us, length us, event | category | flops | bytes accessed | tf_op | source)
XLA Modules:
  0.0 56.2 jit_solution(15880727027268420259)
XLA Ops:
  0.6 53.9 %shard_map.59 = (f32[64,1024]{1,0:T(8,128)}, f32[1,32]{1,0:T(1,128)}) custom-call(f32[512,2048]{1,0:T(8,128)} %sig_hbm.1, f32[32,512]{1,0:T(8,128)} %bitcast.3, s32[4]{0:T(128)} %blk_ref.1), custom_call_target="tpu_custom_call" | custom-call | tf_op jit(solution)/shard_map/pallas_call | solution.py:306
  54.5 1.7 %shard_map.60 = (f32[64,1024]{1,0:T(8,128)}, f32[1,32]{1,0:T(1,128)}) custom-call(f32[64,1024]{1,0:T(8,128)} %get-tuple-element.6.panel_ref, f32[1,32]{1,0:T(1,128)} %get-tuple-element.7.terms_ref, f32[1,32]{1,0:T(1,128)} %bitcast.4), custom_call_target="tpu_custom_call" | custom-call | tf_op jit(solution)/shard_map/pallas_call | solution.py:327

commit v3 on v2

--- a/solution.py
+++ b/solution.py
@@ -250,13 +250,13 @@
     start(3, 5)
     rs_mid(1)
     rs_mid(7)
-    arrive(4, 1)
-    start(4)
     for cp in l1:
         cp.wait_recv()
     for dz in range(1, 8):
         l2cp[dz] = push(ls1.at[(z + dz) % 8], lift.at[dz], l2_s.at[dz], l2_r.at[dz], dev(dz=dz))
     lift[0] = ls1[z]
+    arrive(4, 1)
+    start(4)
     rs_mid(2)
     rs_mid(6)
     rs_mid(3)
@@ -270,26 +270,28 @@
     rs_end(3)
     rs_end(5)
 
+    for cp in pending:
+        if not any(cp is late for late in vacp.values()):
+            cp.wait_send()
     total = va[0]
     for d in range(1, 8):
         vacp[d].wait_recv()
         total = total + va[d]
     vb_src[...] = total
-    vbcp = []
     for i, (dx, dy, dh, dc) in enumerate(plane):
-        vbcp.append(push(vb_src, vb.at[i], vb_s.at[i], vb_r.at[i], dev(dx, dy, 0, dh, dc)))
-    for cp in vbcp:
-        cp.wait_recv()
+        send(vb_src, vb.at[i], vb_s, vb_r, dev(dx, dy, 0, dh, dc))
+    for d in range(1, 8):
+        vacp[d].wait_send()
+    for cp in outs:
+        cp.wait()
+    pltpu.make_async_copy(vb, vb, vb_s).wait()
+    pltpu.make_async_copy(vb, vb, vb_r).wait()
     total = total + jnp.sum(vb[...], axis=0)
     total = jnp.sum(total, axis=0, keepdims=True)
     own = total[:, 0:32]
     for kk in range(1, 4):
         own = jnp.where(k == kk, total[:, kk * 32:kk * 32 + 32], own)
     var_ref[...] = own
-    for cp in outs:
-        cp.wait()
-    for cp in pending:
-        cp.wait_send()
 
 
 def finish(panel_ref, terms_ref, base_ref, cross_ref, var_ref):
@@ -317,7 +319,7 @@
             pltpu.SemaphoreType.DMA,
             dma(16), dma(16), pltpu.SemaphoreType.DMA, pltpu.SemaphoreType.DMA, dma(16), dma(16),
             dma(8), dma(8), dma(8), dma(8),
-            dma(24), dma(24), dma(8), dma(8), dma(8), dma(8), dma(31), dma(31),
+            dma(24), dma(24), dma(8), dma(8), dma(8), dma(8), pltpu.SemaphoreType.DMA, pltpu.SemaphoreType.DMA,
             vm(7, 64, 128), dma(7), dma(7),
         ],
         compiler_params=pltpu.CompilerParams(

time: 56.4 us -> 55.6 us (0.986)
  Pallas kernels: 55.6 us -> 54.8 us
    pallas_call x1, Pallas kernels: 53.9 us -> 53.2 us  [per_device(): pl.pallas_call(kernel, out_shape=(jax.ShapeDtypeStruct((64, 1024), f32),...]
where the time goes in v3:
time: 55.6 us; the launch traced here: 55.5 us
  Pallas kernels  54.8 us (99%)
  between operations  0.64 us (1%)
    pallas_call x1, Pallas kernels, per_device(): pl.pallas_call(kernel, out_shape=(jax.ShapeDtypeStruct((64, 1024), f32),...  53.2 us
    pallas_call x1, Pallas kernels, per_device(): pl.pallas_call(finish, out_shape=(jax.ShapeDtypeStruct((64, 1024), f32),...  1.68 us

profile of v3, /device:TPU:1, one launch (start us, length us, event | category | flops | bytes accessed | tf_op | source)
XLA Modules:
  0.0 55.5 jit_solution(8689445035199357813)
XLA Ops:
  0.6 53.2 %shard_map.59 = (f32[64,1024]{1,0:T(8,128)}, f32[1,32]{1,0:T(1,128)}) custom-call(f32[512,2048]{1,0:T(8,128)} %sig_hbm.1, f32[32,512]{1,0:T(8,128)} %bitcast.3, s32[4]{0:T(128)} %blk_ref.1), custom_call_target="tpu_custom_call" | custom-call | tf_op jit(solution)/shard_map/pallas_call | solution.py:308
  53.8 1.7 %shard_map.60 = (f32[64,1024]{1,0:T(8,128)}, f32[1,32]{1,0:T(1,128)}) custom-call(f32[64,1024]{1,0:T(8,128)} %get-tuple-element.6.panel_ref, f32[1,32]{1,0:T(1,128)} %get-tuple-element.7.terms_ref, f32[1,32]{1,0:T(1,128)} %bitcast.4), custom_call_target="tpu_custom_call" | custom-call | tf_op jit(solution)/shard_map/pallas_call | solution.py:329

commit v4 on v3

--- a/solution.py
+++ b/solution.py
@@ -219,7 +219,7 @@
         outs.append(cp)
         if d:
             l2cp[d].wait_recv()
-        s = jnp.sum((panel * lift[d]).reshape(8, 8, BLK), axis=0)
+        s = jnp.sum((panel * lift[d]).reshape(8, 8, BLK), axis=0).sum(axis=0, keepdims=True)
         if d:
             sv[d] = s
             vacp[d] = push(sv.at[d], va.at[d], va_s.at[d], va_r.at[d], dev(dz=-d))
@@ -286,8 +286,7 @@
         cp.wait()
     pltpu.make_async_copy(vb, vb, vb_s).wait()
     pltpu.make_async_copy(vb, vb, vb_r).wait()
-    total = total + jnp.sum(vb[...], axis=0)
-    total = jnp.sum(total, axis=0, keepdims=True)
+    total = vb_src[...] + jnp.sum(vb[...], axis=0)
     own = total[:, 0:32]
     for kk in range(1, 4):
         own = jnp.where(k == kk, total[:, kk * 32:kk * 32 + 32], own)
@@ -315,7 +314,7 @@
             vm(512, 2048), pltpu.VMEM((512, 1536), jnp.bfloat16), vm(8, 128, 512),
             vm(8, 4, 2, 64, 128), vm(8, 3, 2, 64, 128), vm(8, 4, 64, 128), vm(8, 4, 64, 128),
             vm(8, 64, 128), vm(8, 64, 128), vm(8, 64, 128),
-            vm(8, 8, 128), vm(8, 8, 128), vm(8, 128), vm(31, 8, 128),
+            vm(8, 1, 128), vm(8, 1, 128), vm(1, 128), vm(31, 1, 128),
             pltpu.SemaphoreType.DMA,
             dma(16), dma(16), pltpu.SemaphoreType.DMA, pltpu.SemaphoreType.DMA, dma(16), dma(16),
             dma(8), dma(8), dma(8), dma(8),

time: 55.6 us -> 54.7 us (0.984)
  Pallas kernels: 54.8 us -> 53.9 us
    pallas_call x1, Pallas kernels: 53.2 us -> 52.2 us  [per_device(): pl.pallas_call(kernel, out_shape=(jax.ShapeDtypeStruct((64, 1024), f32),...]
where the time goes in v4:
time: 54.7 us; the launch traced here: 54.5 us
  Pallas kernels  53.9 us (99%)
  between operations  0.64 us (1%)
    pallas_call x1, Pallas kernels, per_device(): pl.pallas_call(kernel, out_shape=(jax.ShapeDtypeStruct((64, 1024), f32),...  52.2 us
    pallas_call x1, Pallas kernels, per_device(): pl.pallas_call(finish, out_shape=(jax.ShapeDtypeStruct((64, 1024), f32),...  1.68 us

profile of v4, /device:TPU:1, one launch (start us, length us, event | category | flops | bytes accessed | tf_op | source)
XLA Modules:
  0.0 54.5 jit_solution(17458349479951488012)
XLA Ops:
  0.6 52.2 %shard_map.59 = (f32[64,1024]{1,0:T(8,128)}, f32[1,32]{1,0:T(1,128)}) custom-call(f32[512,2048]{1,0:T(8,128)} %sig_hbm.1, f32[32,512]{1,0:T(8,128)} %bitcast.3, s32[4]{0:T(128)} %blk_ref.1), custom_call_target="tpu_custom_call" | custom-call | tf_op jit(solution)/shard_map/pallas_call | solution.py:307
  52.8 1.7 %shard_map.60 = (f32[64,1024]{1,0:T(8,128)}, f32[1,32]{1,0:T(1,128)}) custom-call(f32[64,1024]{1,0:T(8,128)} %get-tuple-element.6.panel_ref, f32[1,32]{1,0:T(1,128)} %get-tuple-element.7.terms_ref, f32[1,32]{1,0:T(1,128)} %bitcast.4), custom_call_target="tpu_custom_call" | custom-call | tf_op jit(solution)/shard_map/pallas_call | solution.py:328

commit v5 on v4

--- a/solution.py
+++ b/solution.py
@@ -211,12 +211,6 @@
             for dx in range(1, 4):
                 cps[d, "x", dx].wait_recv()
             panel = stage[d, x] + xr[d, 0, 0] + xr[d, 1, 0] + xr[d, 2, 0]
-        j = (z - d) % 8
-        pan[d] = panel
-        cp = pltpu.make_async_copy(
-            pan.at[d], out_hbm.at[:, pl.ds(pl.multiple_of(j * BLK, BLK), BLK)], out_sem.at[d])
-        cp.start()
-        outs.append(cp)
         if d:
             l2cp[d].wait_recv()
         s = jnp.sum((panel * lift[d]).reshape(8, 8, BLK), axis=0).sum(axis=0, keepdims=True)
@@ -225,6 +219,12 @@
             vacp[d] = push(sv.at[d], va.at[d], va_s.at[d], va_r.at[d], dev(dz=-d))
         else:
             va[0] = s
+        j = (z - d) % 8
+        pan[d] = panel
+        cp = pltpu.make_async_copy(
+            pan.at[d], out_hbm.at[:, pl.ds(pl.multiple_of(j * BLK, BLK), BLK)], out_sem.at[d])
+        cp.start()
+        outs.append(cp)
 
     def start(*ds):
         for d in ds:
@@ -259,11 +259,11 @@
     start(4)
     rs_mid(2)
     rs_mid(6)
-    rs_mid(3)
-    rs_mid(5)
     rs_end(0)
     rs_end(1)
     rs_end(7)
+    rs_mid(3)
+    rs_mid(5)
     rs_end(2)
     rs_end(6)
     rs_end(4)

time: 54.7 us -> 54.5 us (level)
  no operation moved by 1% of the time
where the time goes in v5:
time: 54.5 us; the launch traced here: 54.3 us
  Pallas kernels  53.7 us (99%)
  between operations  0.64 us (1%)
    pallas_call x1, Pallas kernels, per_device(): pl.pallas_call(kernel, out_shape=(jax.ShapeDtypeStruct((64, 1024), f32),...  52 us
    pallas_call x1, Pallas kernels, per_device(): pl.pallas_call(finish, out_shape=(jax.ShapeDtypeStruct((64, 1024), f32),...  1.68 us

profile of v5, /device:TPU:1, one launch (start us, length us, event | category | flops | bytes accessed | tf_op | source)
XLA Modules:
  0.0 54.3 jit_solution(10013680827847774285)
XLA Ops:
  0.6 52.0 %shard_map.59 = (f32[64,1024]{1,0:T(8,128)}, f32[1,32]{1,0:T(1,128)}) custom-call(f32[512,2048]{1,0:T(8,128)} %sig_hbm.1, f32[32,512]{1,0:T(8,128)} %bitcast.3, s32[4]{0:T(128)} %blk_ref.1), custom_call_target="tpu_custom_call" | custom-call | tf_op jit(solution)/shard_map/pallas_call | solution.py:307
  52.7 1.7 %shard_map.60 = (f32[64,1024]{1,0:T(8,128)}, f32[1,32]{1,0:T(1,128)}) custom-call(f32[64,1024]{1,0:T(8,128)} %get-tuple-element.6.panel_ref, f32[1,32]{1,0:T(1,128)} %get-tuple-element.7.terms_ref, f32[1,32]{1,0:T(1,128)} %bitcast.4), custom_call_target="tpu_custom_call" | custom-call | tf_op jit(solution)/shard_map/pallas_call | solution.py:328

commit v6 on v5

--- a/solution.py
+++ b/solution.py
@@ -38,6 +38,9 @@
         )
         cp.start()
         return cp
+
+    def drain(ref, sem):
+        pltpu.make_async_copy(ref, ref, sem).wait()
 
     pending = []
 
@@ -106,7 +109,7 @@
 
     def sibsend(d, op):
         slot = d * 2 + op
-        sibcp[d, op] = push(piece(d, op), piece(d, op), sib_s.at[slot], sib_r.at[slot], dev(dc=1))
+        sibcp[d, op] = push(piece(d, op), piece(d, op), sib_s.at[slot], sib_r.at[d], dev(dc=1))
 
     def arrive(d, op):
         zcp[d, op].wait_recv()
@@ -128,8 +131,7 @@
     sibsend(0, 1)
 
     def sibwait(d):
-        sibcp[d, 0].wait_recv()
-        sibcp[d, 1].wait_recv()
+        drain(front.at[POS[d], 0:64], sib_r.at[d])
 
     l1 = []
     l2cp = {}
@@ -172,19 +174,18 @@
                         if dx + dy:
                             i = dx * 2 + dy - 1
                             to = dev(dx, dy)
-                            cps[d, i] = push(part.at[d, to[0] // 2, to[0] % 2], dr.at[i], d_s.at[i], d_r.at[i], to)
+                            cps[d, i] = push(part.at[d, to[0] // 2, to[0] % 2], dr.at[i], d_s.at[i], d_r.at[0], to)
             elif d in XFIRST:
                 for dx in range(1, 4):
                     cps[d, "x", dx] = push(
                         part.at[d, (x + dx) % 4], xr.at[d, dx - 1],
-                        x_s.at[d * 3 + dx - 1], x_r.at[d * 3 + dx - 1], dev(dx=dx))
+                        x_s.at[d * 3 + dx - 1], x_r.at[d], dev(dx=dx))
             else:
                 cps[d, "y"] = push(part.at[d, :, 1 - yl], yr.at[d], y_s.at[d], y_r.at[d], dev(dy=1))
 
     def rs_mid(d):
         if d in XFIRST:
-            for dx in range(1, 4):
-                cps[d, "x", dx].wait_recv()
+            drain(xr.at[d], x_r.at[d])
             stage[d, 0:2] = part[d, x] + xr[d, 0] + xr[d, 1] + xr[d, 2]
             cps[d, "y"] = push(stage.at[d, 1 - yl], yr.at[d, 0], y_s.at[d], y_r.at[d], dev(dy=1))
         else:
@@ -193,7 +194,7 @@
             for dx in range(1, 4):
                 cps[d, "x", dx] = push(
                     stage.at[d, (x + dx) % 4], xr.at[d, dx - 1, 0],
-                    x_s.at[d * 3 + dx - 1], x_r.at[d * 3 + dx - 1], dev(dx=dx))
+                    x_s.at[d * 3 + dx - 1], x_r.at[d], dev(dx=dx))
 
     vacp = {}
     outs = []
@@ -201,22 +202,21 @@
     def rs_end(d):
         if d == 4:
             panel = part[d, x, yl]
+            drain(dr, d_r.at[0])
             for i in range(7):
-                cps[d, i].wait_recv()
                 panel = panel + dr[i]
         elif d in XFIRST:
             cps[d, "y"].wait_recv()
             panel = stage[d, yl] + yr[d, 0]
         else:
-            for dx in range(1, 4):
-                cps[d, "x", dx].wait_recv()
+            drain(xr.at[d, :, 0], x_r.at[d])
             panel = stage[d, x] + xr[d, 0, 0] + xr[d, 1, 0] + xr[d, 2, 0]
         if d:
             l2cp[d].wait_recv()
         s = jnp.sum((panel * lift[d]).reshape(8, 8, BLK), axis=0).sum(axis=0, keepdims=True)
         if d:
             sv[d] = s
-            vacp[d] = push(sv.at[d], va.at[d], va_s.at[d], va_r.at[d], dev(dz=-d))
+            vacp[d] = push(sv.at[d], va.at[d], va_s.at[d], va_r.at[0], dev(dz=-d))
         else:
             va[0] = s
         j = (z - d) % 8
@@ -274,8 +274,8 @@
         if not any(cp is late for late in vacp.values()):
             cp.wait_send()
     total = va[0]
+    drain(va.at[1:8], va_r.at[0])
     for d in range(1, 8):
-        vacp[d].wait_recv()
         total = total + va[d]
     vb_src[...] = total
     for i, (dx, dy, dh, dc) in enumerate(plane):

time: 54.5 us -> 54.5 us (level)
  no operation moved by 1% of the time
where the time goes in v6:
time: 54.5 us; the launch traced here: 54.3 us
  Pallas kernels  53.7 us (99%)
  between operations  0.64 us (1%)
    pallas_call x1, Pallas kernels, per_device(): pl.pallas_call(kernel, out_shape=(jax.ShapeDtypeStruct((64, 1024), f32),...  52 us
    pallas_call x1, Pallas kernels, per_device(): pl.pallas_call(finish, out_shape=(jax.ShapeDtypeStruct((64, 1024), f32),...  1.68 us

profile of v6, /device:TPU:1, one launch (start us, length us, event | category | flops | bytes accessed | tf_op | source)
XLA Modules:
  0.0 54.3 jit_solution(8845593536224811237)
XLA Ops:
  0.6 52.0 %shard_map.59 = (f32[64,1024]{1,0:T(8,128)}, f32[1,32]{1,0:T(1,128)}) custom-call(f32[512,2048]{1,0:T(8,128)} %sig_hbm.1, f32[32,512]{1,0:T(8,128)} %bitcast.3, s32[4]{0:T(128)} %blk_ref.1), custom_call_target="tpu_custom_call" | custom-call | tf_op jit(solution)/shard_map/pallas_call | solution.py:307
  52.7 1.7 %shard_map.60 = (f32[64,1024]{1,0:T(8,128)}, f32[1,32]{1,0:T(1,128)}) custom-call(f32[64,1024]{1,0:T(8,128)} %get-tuple-element.6.panel_ref, f32[1,32]{1,0:T(1,128)} %get-tuple-element.7.terms_ref, f32[1,32]{1,0:T(1,128)} %bitcast.4), custom_call_target="tpu_custom_call" | custom-call | tf_op jit(solution)/shard_map/pallas_call | solution.py:328
